TPU v7x, 512 devices: a whole 4x4x16 slice. The times are simulated.
512 devices in a mesh: orb: 128 (over x, z, core), aux: 4 (over y).
Axes of the slice: x: 4, y: 4, z: 16, core: 2. Of those that a mesh axis runs over, the one named last changes fastest.
Arguments:
- orbital_factors: bfloat16 [512, 384, 1536], P('orb', None, 'aux'), may hold values from -1 to 1
- metric_factor: bfloat16 [1536, 1536], P(None, 'aux'), may hold values from -0.15625 to 0.15625
- occ_energy: float32 [512], replicated, may hold values from -2 to -0.3
- vir_energy: float32 [384], replicated, may hold values from 0.2 to 3
- pair_list: int32 [768, 2], P('orb'), may hold values from 0 to 511, as said below
Outputs:
- gradient_factors: bfloat16 [512, 384, 1536], P('orb', None, 'aux')
Inputs may be any that keep to these rules, and one draw needn't show every extreme that they name: `pair_list`: row r belongs to device r // 6 of orb, where orbital o is owned by device o // 4; its first entry is an orbital of that device; its second is an orbital of the device (r % 6) % 3 - 1 places further along orb, or of the row's own device where that place lies outside orb.
All inputs are finite; a program needn't handle non-finite values.
Results may differ from a plain program's by a relative error of at most 0.0083.
Values may be sent and summed in bfloat16 or wider, within the bound.
A program may use at most 64 MiB of HBM per device.

v0:
```python
import jax
import jax.numpy as jnp
from jax import lax
from jax.sharding import PartitionSpec as P


def with_halo(array, sides, width):
    for axis, dim in sides:
        size, length = (lax.axis_size(axis), array.shape[dim])
        up = [(i, (i + 1) % size) for i in range(size - 1)]
        down = [(j, i) for i, j in up]
        last = lax.slice_in_dim(array, length - width, length, axis=dim)
        initial = lax.slice_in_dim(array, 0, width, axis=dim)
        before = lax.ppermute(last, axis, up)
        after = lax.ppermute(initial, axis, down)
        array = jnp.concatenate([before, array, after], axis=dim)
    return array


def split_up(array, dim, length):
    lengths = array.shape
    tiles = array.reshape(*lengths[:dim], length, lengths[dim] // length, *lengths[dim + 1 :])
    return jnp.moveaxis(tiles, dim, 0)


def sent_and_summed(array, axis, dim):
    length = lax.axis_size(axis)
    tiles = lax.all_to_all(split_up(array, dim, length), axis, 0, 0, tiled=True)
    return jnp.sum(tiles.astype(jnp.float32), axis=0)


def from_everyone(array, axis):
    length = lax.axis_size(axis)
    return lax.all_to_all(
        jnp.broadcast_to(array[None], (length, *array.shape)), axis, 0, 0, tiled=True
    )


def in_order(tiles, dim):
    tiles = jnp.moveaxis(tiles, 0, dim)
    lengths = tiles.shape
    return tiles.reshape(*lengths[:dim], lengths[dim] * lengths[dim + 1], *lengths[dim + 2 :])


def collect(array, axis, dim):
    tiles = from_everyone(array, axis)
    return in_order(tiles, dim)


def from_behind(value, axis, steps):
    count = lax.axis_size(axis)
    initial, last = (max(0, -steps), min(count, count - steps))
    return lax.ppermute(value, axis, [(source, source + steps) for source in range(initial, last)])


def local(orbital_factors, metric_factor, occ_energy, vir_energy, pair_list):
    owned = orbital_factors.shape[0]
    virtuals = orbital_factors.shape[1]
    widened = with_halo(orbital_factors, (("orb", 0),), owned)
    own_start = lax.axis_index("orb") * owned
    offset = own_start - owned
    left_index = pair_list[:, 0] - offset
    right_index = pair_list[:, 1] - offset
    left_blocks = jnp.take(widened, left_index, axis=0)
    right_blocks = jnp.take(widened, right_index, axis=0)
    partial_value = jnp.einsum(
        "nax,nbx->nab", left_blocks, right_blocks, preferred_element_type=jnp.float32
    )
    orbitals = jnp.arange(occ_energy.shape[0], dtype=jnp.int32)
    left_energy = jnp.sum(
        jnp.where(pair_list[:, 0, None] == orbitals[None, :], occ_energy[None, :], 0.0), axis=1
    )
    right_energy = jnp.sum(
        jnp.where(pair_list[:, 1, None] == orbitals[None, :], occ_energy[None, :], 0.0), axis=1
    )
    pair_energy = left_energy + right_energy
    shares = sent_and_summed(partial_value.astype(jnp.bfloat16), "aux", 1)
    row_count = shares.shape[1]
    row_start = lax.axis_index("aux") * row_count
    vir_rows = lax.dynamic_slice_in_dim(vir_energy, row_start, row_count)
    denominator = pair_energy[:, None, None] - vir_rows[None, :, None] - vir_energy[None, None, :]
    amplitude_share = (shares / denominator).astype(jnp.bfloat16)
    amplitudes = collect(amplitude_share, "aux", 1)
    left_terms = jnp.einsum(
        "nab,nbx->nax", amplitudes, right_blocks, preferred_element_type=jnp.float32
    )
    right_terms = jnp.einsum(
        "nab,nax->nbx", amplitudes, left_blocks, preferred_element_type=jnp.float32
    )
    pair_count = left_terms.shape[0]
    term_rows = jnp.concatenate([left_terms, right_terms], axis=0).reshape(2 * pair_count, -1)
    slot_ids = jnp.arange(3 * owned, dtype=jnp.int32)
    targets = jnp.concatenate([left_index, right_index], axis=0)
    selector = (targets[:, None] == slot_ids[None, :]).astype(jnp.float32)
    summed = jnp.einsum("nk,nm->km", selector, term_rows, precision=lax.Precision.HIGHEST)
    summed = summed.reshape(3 * owned, virtuals, -1)

    def outgoing(first_slot, receiver_start):
        chosen = pair_list[first_slot::3]
        first_ids = chosen[:, 0] - own_start
        second_ids = chosen[:, 1] - receiver_start
        id_pairs = jnp.stack([first_ids, second_ids], axis=1).astype(jnp.bfloat16)
        return (amplitudes[first_slot::3], id_pairs)

    def arrived_terms(amplitude_set, id_pairs, base):
        id_values = id_pairs.astype(jnp.int32)
        block_ids = base + id_values[:, 0]
        blocks = jnp.take(widened, block_ids, axis=0)
        terms = jnp.einsum(
            "nab,nax->nbx", amplitude_set, blocks, preferred_element_type=jnp.float32
        )
        owner_slots = jnp.arange(owned, dtype=jnp.int32)
        picker = (id_values[:, 1, None] == owner_slots[None, :]).astype(jnp.float32)
        return jnp.einsum("nk,nbx->kbx", picker, terms, precision=lax.Precision.HIGHEST)

    left_amps, left_ids = outgoing(0, own_start - owned)
    right_amps, right_ids = outgoing(2, own_start + owned)
    came_right_amps, came_right_ids = from_behind((left_amps, left_ids), "orb", -1)
    came_left_amps, came_left_ids = from_behind((right_amps, right_ids), "orb", 1)
    density_sum = summed[owned : 2 * owned]
    density_sum = density_sum + arrived_terms(came_right_amps, came_right_ids, 2 * owned)
    density_sum = density_sum + arrived_terms(came_left_amps, came_left_ids, 0)
    density = density_sum.astype(jnp.bfloat16)
    shard_piece = lax.all_gather(density, "aux", axis=2, tiled=True)
    width = shard_piece.shape[2]
    flat_piece = shard_piece.reshape(-1, width)
    result = jnp.dot(flat_piece, metric_factor, preferred_element_type=jnp.float32)
    return result.astype(jnp.bfloat16).reshape(owned, virtuals, -1)


def solution(mesh):
    placed = (P("orb", None, "aux"), P(None, "aux"), P(), P(), P("orb", None))
    return jax.shard_map(
        local, mesh=mesh, in_specs=placed, out_specs=P("orb", None, "aux"), check_vma=False
    )
```

profile of v0, /device:TPU:6, one launch (start us, length us, event | category | flops | bytes accessed | tf_op | source)
XLA Modules:
  0.0 220.7 jit_solution(16919540255938241089)
XLA Ops:
  6.5 2.0 collective-permute-start
  8.6 11.1 %collective-permute-start.1 = (bf16[4,384,384]{2,1,0:T(8,128)(2,1)}, bf16[4,384,384]{2,1,0:T(8,128)(2,1)}, u32[]{:S(2)}, u32[]{:S(2)}) collective-permute-start(bf16[4,384,384]{2,1,0:T(8,128)(2,1)} %param.9), channel_id=1, source_target_pairs={{4,0},{8,4},{12,8},{16,12},{20,16},{24,20},{28,24},{32,28},{36,32}... | collective-permute-start | bytes 3538952 | tf_op jit(solution)/shard_map/ppermute | solution.py:15
  20.5 11.5 %collective-permute-done = bf16[4,384,384]{2,1,0:T(8,128)(2,1)} collective-permute-done((bf16[4,384,384]{2,1,0:T(8,128)(2,1)}, bf16[4,384,384]{2,1,0:T(8,128)(2,1)}, u32[]{:S(2)}, u32[]{:S(2)}) %collective-permute-start) | collective-permute-done | bytes 1179680 | tf_op jit(solution)/shard_map/ppermute | solution.py:14
  32.0 2.4 %constant_dynamic-update-slice_fusion.2 = bf16[12,384,384]{2,1,0:T(8,128)(2,1)} fusion(bf16[4,384,384]{2,1,0:T(8,128)(2,1)} %collective-permute-done), kind=kLoop, calls=%fused_computation.34 | loop fusion | bytes 2359296
  35.5 2.4 %constant_dynamic-update-slice_fusion = bf16[12,384,384]{2,1,0:T(8,128)(2,1)} fusion(bf16[12,384,384]{2,1,0:T(8,128)(2,1)} %constant_dynamic-update-slice_fusion.1, bf16[4,384,384]{2,1,0:T(8,128)(2,1)} %collective-permute-done.1), kind=kLoop, calls=%fused_computation.32 | loop fusion | bytes 2359296 | tf_op jit(solution)/shard_map/concatenate | solution.py:16
  37.9 3.0 %gather_fusion.1 = bf16[6,384,384]{2,1,0:T(8,128)(2,1)S(1)} fusion(bf16[12,384,384]{2,1,0:T(8,128)(2,1)} %constant_dynamic-update-slice_fusion, s32[1024]{0:T(1024)S(1)} %pad_clamp_fusion.2), kind=kCustom, calls=%fused_computation.2.clone | custom fusion | bytes 3538968 | tf_op jit(solution)/shard_map/jit(_take)/gather | solution.py:65
  40.9 4.1 %gather_fusion = bf16[6,384,384]{2,1,0:T(8,128)(2,1)} fusion(bf16[12,384,384]{2,1,0:T(8,128)(2,1)} %constant_dynamic-update-slice_fusion, s32[1024]{0:T(1024)S(1)} %pad_clamp_fusion.3), kind=kCustom, calls=%fused_computation.clone | custom fusion | bytes 3538968 | tf_op jit(solution)/shard_map/jit(_take)/gather | solution.py:64
  45.0 2.9 %convolution_convert_fusion.1 = bf16[6,384,384]{2,1,0:T(8,128)(2,1)S(1)} fusion(bf16[6,384,384]{2,1,0:T(8,128)(2,1)} %gather_fusion, pred[6]{0:T(512)(128)(4,1)S(1)} %get-tuple-element.25, bf16[6,384,384]{2,1,0:T(8,128)(2,1)S(1)} %gather_fusion.1, pred[6]{0:T(512)(128)(4,1)S(1)} %get-tuple-element.13), kind=kOutput, calls=%fused_computation.11 | convolution fusion | flops 682131456 | bytes 5308428 | tf_op jit(solution)/shard_map/nax,nbx->nab/dot_general | solution.py:66
  47.9 1.5 copy.38
  49.4 4.6 %all-to-all-start = ((bf16[4,6,96,384]{3,2,1,0:T(8,128)(2,1)}), bf16[4,6,96,384]{3,2,1,0:T(8,128)(2,1)}, u32[]{:S(2)}, u32[]{:S(2)}) async-start(bf16[4,6,96,384]{3,2,1,0:T(8,128)(2,1)} %bitcast.51), calls=%async_computation | async-start | bytes 3538944 | tf_op jit(solution)/shard_map/all_to_all | solution.py:28
  54.2 4.1 %collective-permute-start.2 = (bf16[2,2]{0,1:T(2,128)(2,1)S(1)}, bf16[2,2]{0,1:T(2,128)(2,1)S(1)}, u32[]{:S(2)}, u32[]{:S(2)}) collective-permute-start(bf16[2,2]{0,1:T(2,128)(2,1)S(1)} %pad_maximum_fusion.1), channel_id=1, source_target_pairs={{4,0},{8,4},{12,8},{16,12},{20,16},{24,20},{28,24},{32,28},{36,32}... | collective-permute-start | bytes 32 | tf_op jit(solution)/shard_map/ppermute | solution.py:53
  58.7 11.8 %all-to-all-done = bf16[4,6,96,384]{3,2,1,0:T(8,128)(2,1)} async-done(((bf16[4,6,96,384]{3,2,1,0:T(8,128)(2,1)}), bf16[4,6,96,384]{3,2,1,0:T(8,128)(2,1)}, u32[]{:S(2)}, u32[]{:S(2)}) %all-to-all-start) | async-done | bytes 1769504 | tf_op jit(solution)/shard_map/all_to_all | solution.py:28
  70.5 1.8 convert_reduce_fusion
  72.5 1.5 broadcast_in_dim.53
  74.0 4.4 %all-to-all-start.1 = ((bf16[4,6,96,384]{3,2,1,0:T(8,128)(2,1)}), bf16[4,6,96,384]{3,2,1,0:T(8,128)(2,1)}, u32[]{:S(2)}, u32[]{:S(2)}) async-start(bf16[4,6,96,384]{3,2,1,0:T(8,128)(2,1)} %broadcast_in_dim.53), calls=%async_computation.1 | async-start | bytes 3538944 | tf_op jit(solution)/shard_map/all_to_all | solution.py:34
  78.4 1.9 collective-permute-start.4
  81.0 8.9 %collective-permute-done.4 = bf16[2,2]{0,1:T(2,128)(2,1)S(1)} collective-permute-done((bf16[2,2]{0,1:T(2,128)(2,1)S(1)}, bf16[2,2]{0,1:T(2,128)(2,1)S(1)}, u32[]{:S(2)}, u32[]{:S(2)}) %collective-permute-start.4) | collective-permute-done | bytes 40 | tf_op jit(solution)/shard_map/ppermute | solution.py:53
  92.2 2.7 %gather_fusion.3 = bf16[2,384,384]{2,1,0:T(8,128)(2,1)S(1)} fusion(bf16[12,384,384]{2,1,0:T(8,128)(2,1)} %constant_dynamic-update-slice_fusion, s32[1024]{0:T(1024)S(1)} %pad_clamp_fusion), kind=kCustom, calls=%fused_computation.3.clone | custom fusion | bytes 1179656 | tf_op jit(solution)/shard_map/jit(_take)/gather | solution.py:108
  94.9 3.4 %gather_fusion.2 = bf16[2,384,384]{2,1,0:T(8,128)(2,1)} fusion(bf16[12,384,384]{2,1,0:T(8,128)(2,1)} %constant_dynamic-update-slice_fusion, s32[1024]{0:T(1024)S(1)} %pad_clamp_fusion.1), kind=kCustom, calls=%fused_computation.1.clone | custom fusion | bytes 1179656 | tf_op jit(solution)/shard_map/jit(_take)/gather | solution.py:108
  98.3 1.7 copy.21
  100.2 1.3 copy-done.1
  101.5 1.3 fusion.3
  104.2 1.9 collective-permute-start.5
  106.1 12.3 %collective-permute-start.3 = (bf16[2,384,384]{2,1,0:T(8,128)(2,1)S(1)}, bf16[2,384,384]{2,1,0:T(8,128)(2,1)S(1)}, u32[]{:S(2)}, u32[]{:S(2)}) collective-permute-start(bf16[2,384,384]{2,1,0:T(8,128)(2,1)S(1)} %get-tuple-element.18), channel_id=1, source_target_pairs={{4,0},{8,4},{12,8},{16,12},{20,16},{24,20},{28,24},{32,28},{36,32}... | collective-permute-start | bytes 1769480 | tf_op jit(solution)/shard_map/ppermute | solution.py:53
  118.9 4.6 %pad.12 = f32[16,384,384]{2,1,0:T(8,128)} pad(f32[12,384,384]{2,1,0:T(8,128)S(1)} %pad_maximum_fusion, f32[]{:T(128)} %constant.7.clone.1), padding=0_4x0_0x0_0 | pad | bytes 16515076
  123.5 9.1 %copy.32 = f32[2,8,384,384]{3,1,2,0:T(8,128)S(1)} copy(f32[2,8,384,384]{3,2,1,0:T(8,128)} %bitcast.46) | data formatting | bytes 18874368
  132.7 3.9 %fusion.13 = f32[4,147456]{1,0:T(4,128)S(1)} fusion(f32[12,147456]{1,0:T(8,128)S(1)} %bitcast.45, s32[12]{0:T(128)S(1)} %copy-done.7), kind=kOutput, calls=%fused_computation.31 | convolution fusion | flops 84934752 | bytes 9437232 | tf_op jit(solution)/shard_map/nk,nm->km/dot_general | solution.py:95
  137.4 3.6 %fusion.1 = f32[4,384,384]{2,0,1:T(4,128)S(1)} fusion(f32[2,384,384]{2,1,0:T(8,128)S(1)} %fusion.7, s32[2]{0:T(128)S(1)} %copy-done.11), kind=kOutput, calls=%fused_computation.13 | convolution fusion | flops 14155784 | bytes 3538952 | tf_op jit(solution)/shard_map/nk,nbx->kbx/dot_general | solution.py:114
  141.6 5.2 %add_convert_fusion = bf16[4,384,384]{2,0,1:T(4,128)(2,1)} fusion(f32[4,384,384]{2,0,1:T(4,128)S(1)} %bitcast.50, f32[4,384,384]{2,0,1:T(4,128)S(1)} %fusion.1, f32[2,384,384]{2,1,0:T(8,128)S(1)} %fusion.5, s32[2]{0:T(128)S(1)} %copy-done.9), kind=kOutput, calls=%fused_computation.7 | convolution fusion | flops 15925256 | bytes 7077896 | tf_op jit(solution)/shard_map/nk,nbx->kbx/dot_general | solution.py:114
  146.8 60.1 %all-gather.2.cloned.1.call-done = bf16[4,384,1536]{2,0,1:T(4,128)(2,1)} async-done(((bf16[4,384,384]{2,0,1:T(4,128)(2,1)}), bf16[4,384,1536]{2,0,1:T(4,128)(2,1)}) %all-gather.2.cloned.1.call-update) | async-done | bytes 4718608 | tf_op jit(solution)/shard_map/all_gather | solution.py:124
  206.9 3.2 %copy.28 = bf16[4,384,1536]{2,1,0:T(8,128)(2,1)S(1)} copy(bf16[4,384,1536]{2,0,1:T(4,128)(2,1)} %all-gather.2.cloned.1.call-done) | data formatting | bytes 9437184 | tf_op jit(solution)/shard_map/all_gather | solution.py:124
  210.2 3.7 %convolution_convert_fusion = bf16[1536,384]{1,0:T(8,128)(2,1)} fusion(bf16[1536,1536]{1,0:T(8,128)(2,1)S(1)} %bitcast.52, bf16[1536,384]{1,0:T(8,128)(2,1)S(1)} %copy-done), kind=kOutput, calls=%fused_computation.6 | convolution fusion | flops 1812529152 | bytes 7077888 | tf_op jit(solution)/shard_map/dot_general | solution.py:127
  (60 shorter events, 8.9 us)
Async XLA Ops:
  6.5 203.6 %copy-start = (bf16[1536,384]{1,0:T(8,128)(2,1)S(1)}, bf16[1536,384]{1,0:T(8,128)(2,1)}, u32[]{:S(2)}) copy-start(bf16[1536,384]{1,0:T(8,128)(2,1)} %param.10) | copy-start | bytes 3538948
  6.5 27.8 %copy-start.3 = (bf16[4,384,384]{2,1,0:T(8,128)(2,1)S(1)}, bf16[4,384,384]{2,1,0:T(8,128)(2,1)}, u32[]{:S(2)}) copy-start(bf16[4,384,384]{2,1,0:T(8,128)(2,1)} %param.9) | copy-start | bytes 3538948
  6.5 25.4 %collective-permute-start = (bf16[4,384,384]{2,1,0:T(8,128)(2,1)}, bf16[4,384,384]{2,1,0:T(8,128)(2,1)}, u32[]{:S(2)}, u32[]{:S(2)}) collective-permute-start(bf16[4,384,384]{2,1,0:T(8,128)(2,1)} %param.9), channel_id=1, source_target_pairs={{0,4},{4,8},{8,12},{12,16},{16,20},{20,24},{24,28},{28,32},{32,36}... | collective-permute-start | bytes 3538952 | tf_op jit(solution)/shard_map/ppermute | solution.py:14
  8.6 26.9 %collective-permute-start.1 = (bf16[4,384,384]{2,1,0:T(8,128)(2,1)}, bf16[4,384,384]{2,1,0:T(8,128)(2,1)}, u32[]{:S(2)}, u32[]{:S(2)}) collective-permute-start(bf16[4,384,384]{2,1,0:T(8,128)(2,1)} %param.9), channel_id=1, source_target_pairs={{4,0},{8,4},{12,8},{16,12},{20,16},{24,20},{28,24},{32,28},{36,32}... | collective-permute-start | bytes 3538952 | tf_op jit(solution)/shard_map/ppermute | solution.py:15
  49.4 4.6 %copy-start.4 = (s32[6,2]{0,1:T(2,128)S(1)}, s32[6,2]{0,1:T(2,128)}, u32[]{:S(2)}) copy-start(s32[6,2]{0,1:T(2,128)} %param.13) | copy-start | bytes 148
  49.4 8.9 %copy-start.5 = (f32[384]{0:T(512)S(1)}, f32[384]{0:T(512)}, u32[]{:S(2)}) copy-start(f32[384]{0:T(512)} %param.12) | copy-start | bytes 4612
  49.4 9.0 %copy-start.6 = (f32[512]{0:T(512)S(1)}, f32[512]{0:T(512)}, u32[]{:S(2)}) copy-start(f32[512]{0:T(512)} %param.11) | copy-start | bytes 6148
  49.4 21.1 %all-to-all-start = ((bf16[4,6,96,384]{3,2,1,0:T(8,128)(2,1)}), bf16[4,6,96,384]{3,2,1,0:T(8,128)(2,1)}, u32[]{:S(2)}, u32[]{:S(2)}) async-start(bf16[4,6,96,384]{3,2,1,0:T(8,128)(2,1)} %bitcast.51), calls=%async_computation | async-start | bytes 3538944 | tf_op jit(solution)/shard_map/all_to_all | solution.py:28
  54.2 26.8 %collective-permute-start.2 = (bf16[2,2]{0,1:T(2,128)(2,1)S(1)}, bf16[2,2]{0,1:T(2,128)(2,1)S(1)}, u32[]{:S(2)}, u32[]{:S(2)}) collective-permute-start(bf16[2,2]{0,1:T(2,128)(2,1)S(1)} %pad_maximum_fusion.1), channel_id=1, source_target_pairs={{4,0},{8,4},{12,8},{16,12},{20,16},{24,20},{28,24},{32,28},{36,32}... | collective-permute-start | bytes 32 | tf_op jit(solution)/shard_map/ppermute | solution.py:53
  74.0 24.3 %all-to-all-start.1 = ((bf16[4,6,96,384]{3,2,1,0:T(8,128)(2,1)}), bf16[4,6,96,384]{3,2,1,0:T(8,128)(2,1)}, u32[]{:S(2)}, u32[]{:S(2)}) async-start(bf16[4,6,96,384]{3,2,1,0:T(8,128)(2,1)} %broadcast_in_dim.53), calls=%async_computation.1 | async-start | bytes 3538944 | tf_op jit(solution)/shard_map/all_to_all | solution.py:34
  78.4 128.5 %all-gather.2.cloned.1.call-start = ((), (), s32[]{:S(2)}) async-start(), calls=%async_computation.2 | async-start | bytes 5898240 | tf_op jit(solution)/shard_map/all_gather | solution.py:124
  78.4 11.5 %collective-permute-start.4 = (bf16[2,2]{0,1:T(2,128)(2,1)S(1)}, bf16[2,2]{0,1:T(2,128)(2,1)S(1)}, u32[]{:S(2)}, u32[]{:S(2)}) collective-permute-start(bf16[2,2]{0,1:T(2,128)(2,1)S(1)} %pad_maximum_fusion.2), channel_id=1, source_target_pairs={{0,4},{4,8},{8,12},{12,16},{16,20},{20,24},{24,28},{28,32},{32,36}... | collective-permute-start | bytes 32 | tf_op jit(solution)/shard_map/ppermute | solution.py:53
  100.0 1.5 copy-start.1
  104.2 36.8 %collective-permute-start.5 = (bf16[2,384,384]{2,1,0:T(8,128)(2,1)S(1)}, bf16[2,384,384]{2,1,0:T(8,128)(2,1)S(1)}, u32[]{:S(2)}, u32[]{:S(2)}) collective-permute-start(bf16[2,384,384]{2,1,0:T(8,128)(2,1)S(1)} %get-tuple-element.17), channel_id=1, source_target_pairs={{0,4},{4,8},{8,12},{12,16},{16,20},{20,24},{24,28},{28,32},{32,36}... | collective-permute-start | bytes 1769480 | tf_op jit(solution)/shard_map/ppermute | solution.py:53
  106.1 30.6 %collective-permute-start.3 = (bf16[2,384,384]{2,1,0:T(8,128)(2,1)S(1)}, bf16[2,384,384]{2,1,0:T(8,128)(2,1)S(1)}, u32[]{:S(2)}, u32[]{:S(2)}) collective-permute-start(bf16[2,384,384]{2,1,0:T(8,128)(2,1)S(1)} %get-tuple-element.18), channel_id=1, source_target_pairs={{4,0},{8,4},{12,8},{16,12},{20,16},{24,20},{28,24},{32,28},{36,32}... | collective-permute-start | bytes 1769480 | tf_op jit(solution)/shard_map/ppermute | solution.py:53
  123.5 9.1 %copy-start.7 = (s32[12]{0:T(128)S(1)}, s32[12]{0:T(128)}, u32[]{:S(2)}) copy-start(s32[12]{0:T(128)} %pad_add_fusion) | copy-start | bytes 148
  132.7 4.0 %copy-start.2 = (bf16[2,384,384]{2,1,0:T(8,128)(2,1)S(1)}, bf16[2,384,384]{2,1,0:T(8,128)(2,1)}, u32[]{:S(2)}) copy-start(bf16[2,384,384]{2,1,0:T(8,128)(2,1)} %gather_fusion.2) | copy-start | bytes 1769476
  132.7 4.0 %copy-start.10 = (pred[2]{0:T(512)(128)(4,1)S(1)}, pred[2]{0:T(512)(128)(4,1)}, u32[]{:S(2)}) copy-start(pred[2]{0:T(512)(128)(4,1)} %get-tuple-element.11) | copy-start | bytes 10
  136.7 0.7 copy-start.11
  137.4 3.7 %copy-start.8 = (pred[2]{0:T(512)(128)(4,1)S(1)}, pred[2]{0:T(512)(128)(4,1)}, u32[]{:S(2)}) copy-start(pred[2]{0:T(512)(128)(4,1)} %get-tuple-element.9) | copy-start | bytes 10
  141.0 0.7 copy-start.9
Sparse Core Ops, SparseCore 0:
  147.0 59.9 all-gather.1
where the time goes:
time: 222 us; the launch traced here: 221 us
  waiting for transfers between devices  92.3 us (42%)
  local copies, waits for them, and re-layouts  43.8 us (20%)
  starting transfers between devices  42.3 us (19%)
  matrix products  23.2 us (10%)
  between operations  13.7 us (6%)
  other arithmetic  5.4 us (2%)
    all_gather x1, waiting for transfers between devices, local(): shard_piece = lax.all_gather(density, 'aux', axis=2, tiled=True)  60.1 us
    ppermute x4, starting transfers between devices, from_behind(): lax.ppermute(value, axis, [(source, source + steps) for source in range(i...  20.2 us
    unnamed x28, local copies, waits for them, and re-layouts  18.7 us
    all_to_all x1, waiting for transfers between devices, sent_and_summed(): tiles = lax.all_to_all(split_up(array, dim, length), axis, 0, 0, tiled=True)  11.8 us
    ppermute x1, waiting for transfers between devices, with_halo(): before = lax.ppermute(last, axis, up)  11.5 us
    ppermute x1, starting transfers between devices, with_halo(): after = lax.ppermute(initial, axis, down)  11.1 us
    ppermute x4, waiting for transfers between devices, from_behind(): lax.ppermute(value, axis, [(source, source + steps) for source in range(i...  8.94 us
    dot_general x2, matrix products, arrived_terms(): jnp.einsum('nk,nbx->kbx', picker, terms, precision=lax.Precision.HIGHEST)  8.79 us
  transfers between devices with their start and end apart: 9, of which 4 were waited for; matrix products, arithmetic and copies ran while one was open for 18% of the time, Pallas kernels for 0%

commit v1 on v0

v1 whole, which is shorter than its diff:
```python
import functools

import jax
import jax.numpy as jnp
from jax import lax
from jax.experimental import pallas as pl
from jax.experimental.pallas import tpu as pltpu
from jax.sharding import PartitionSpec as P

MESH = pl.DeviceIdType.MESH
F32 = jnp.float32
BF16 = jnp.bfloat16
CHUNKS = 4


def dot(a, b):
    return lax.dot_general(a, b, (((1,), (0,)), ((), ())), preferred_element_type=F32)


def dot_nt(a, b):
    return lax.dot_general(a, b, (((1,), (1,)), ((), ())), preferred_element_type=F32)


def dot_tn(a, b):
    return lax.dot_general(a, b, (((0,), (0,)), ((), ())), preferred_element_type=F32)


def kernel(
    n_orb,
    b_hbm,
    m_hbm,
    occ,
    vir,
    pairs,
    out,
    bown,
    m,
    gathered,
    halo_l,
    halo_r,
    stage_l,
    stage_r,
    got_l,
    got_r,
    ids,
    acc_i,
    recip,
    acc_c,
    cb,
    amp,
    term,
    total,
    tsend_l,
    tsend_r,
    trecv_l,
    trecv_r,
    load_sem,
    id_send,
    id_recv,
    y_send,
    y_recv,
    z_send,
    z_recv,
    t_send,
    t_recv,
):
    owned, virt, width = bown.shape
    rows = virt // CHUNKS
    half = CHUNKS // 2
    o = lax.axis_index("orb")
    y = lax.axis_index("aux")
    has_l = o > 0
    has_r = o < n_orb - 1
    up, down = lax.rem(y + 1, 4), lax.rem(y + 3, 4)
    to_up, to_down = (o, up), (o, down)
    to_l, to_r = (o - 1, y), (o + 1, y)

    load_b = pltpu.make_async_copy(b_hbm, bown, load_sem.at[0])
    load_m = pltpu.make_async_copy(m_hbm, m, load_sem.at[1])
    load_b.start()
    load_m.start()

    barrier = pltpu.get_barrier_semaphore()
    pl.semaphore_signal(barrier, inc=1, device_id=to_up, device_id_type=MESH)
    pl.semaphore_signal(barrier, inc=1, device_id=to_down, device_id_type=MESH)

    @pl.when(has_l)
    def _():
        pl.semaphore_signal(barrier, inc=1, device_id=to_l, device_id_type=MESH)

    @pl.when(has_r)
    def _():
        pl.semaphore_signal(barrier, inc=1, device_id=to_r, device_id_type=MESH)

    pl.semaphore_wait(barrier, 2 + has_l.astype(jnp.int32) + has_r.astype(jnp.int32))
    load_b.wait()

    def remote(src, dst, send, recv, device):
        return pltpu.make_async_remote_copy(
            src_ref=src, dst_ref=dst, send_sem=send, recv_sem=recv, device_id=device, device_id_type=MESH
        )

    ids_l = remote(pairs, got_r, id_send.at[0], id_recv.at[0], to_l)
    ids_r = remote(pairs, got_l, id_send.at[1], id_recv.at[1], to_r)

    @pl.when(has_l)
    def _():
        ids_l.start()

    @pl.when(has_r)
    def _():
        ids_r.start()

    def row_span(c):
        return pl.ds(c * rows, rows)

    send_up = [
        remote(bown.at[:, row_span(c)], gathered[0][c], y_send.at[0, c], y_recv.at[0, c], to_up) for c in range(CHUNKS)
    ]
    send_down = [
        remote(bown.at[:, row_span(c)], gathered[1][c], y_send.at[1, c], y_recv.at[1, c], to_down) for c in range(CHUNKS)
    ]
    pass_on = [
        remote(gathered[0][c], gathered[2][c], y_send.at[2, c], y_recv.at[2, c], to_up)
        if c < half
        else remote(gathered[1][c], gathered[2][c], y_send.at[2, c], y_recv.at[2, c], to_down)
        for c in range(CHUNKS)
    ]
    up_order = list(range(CHUNKS))
    down_order = up_order[half:] + up_order[:half]
    for cu, cd in zip(up_order, down_order):
        send_up[cu].start()
        send_down[cd].start()

    @pl.when(has_l)
    def _():
        ids_r.wait_recv()
        for q in range(2):
            ids[q] = lax.rem(got_l[3 * q + 2, 1], owned)

    @pl.when(jnp.logical_not(has_l))
    def _():
        for q in range(2):
            ids[q] = lax.rem(pairs[3 * q, 1], owned)

    @pl.when(has_r)
    def _():
        ids_l.wait_recv()
        for q in range(2):
            ids[2 + q] = lax.rem(got_r[3 * q, 1], owned)

    @pl.when(jnp.logical_not(has_r))
    def _():
        for q in range(2):
            ids[2 + q] = lax.rem(pairs[3 * q + 2, 1], owned)

    def halo_left(s, c):
        span = row_span(c)
        return remote(stage_l.at[s, :, span], halo_r.at[s, :, span], z_send.at[0, s, c], z_recv.at[0, s, c], to_l)

    def halo_right(s, c):
        span = row_span(c)
        return remote(stage_r.at[s, :, span], halo_l.at[s, :, span], z_send.at[1, s, c], z_recv.at[1, s, c], to_r)

    def pick(s, c, k):
        return bown[k, row_span(c), :] if s == 0 else gathered[s - 1][c][k]

    def stage(s, c):
        span = row_span(c)

        @pl.when(has_l)
        def _():
            for q in range(2):
                stage_l[s, q, span, :] = pick(s, c, ids[q])
            halo_left(s, c).start()

        @pl.when(jnp.logical_not(has_l))
        def _():
            for q in range(2):
                halo_l[s, q, span, :] = pick(s, c, ids[q])

        @pl.when(has_r)
        def _():
            for q in range(2):
                stage_r[s, q, span, :] = pick(s, c, ids[2 + q])
            halo_right(s, c).start()

        @pl.when(jnp.logical_not(has_r))
        def _():
            for q in range(2):
                halo_r[s, q, span, :] = pick(s, c, ids[2 + q])

    def halo_wait(s):
        for c in range(CHUNKS):
            @pl.when(has_r)
            def _():
                halo_left(s, c).wait_recv()

            @pl.when(has_l)
            def _():
                halo_right(s, c).wait_recv()

    def own(s, k):
        return bown[k] if s == 0 else jnp.concatenate([g[k] for g in gathered[s - 1]], axis=0)

    def metric_rows(s):
        source = lax.rem(y + (0, 3, 1, 2)[s], 4)
        return m[pl.ds(pl.multiple_of(source * width, width), width), :]

    def put_c(s, slot, value):
        if s == 0:
            acc_c[slot] = value
        elif s < 3:
            acc_c[slot] += value
        else:
            cb[slot] = (acc_c[slot] + value).astype(BF16)

    def put_i(s, slot, value):
        if s == 0:
            acc_i[slot] = value
        elif s < 3:
            acc_i[slot] += value
        else:
            amp[slot] = ((acc_i[slot] + value) * recip[slot]).astype(BF16)

    def compute_own(s):
        @pl.loop(0, owned)
        def _(k):
            put_c(s, k, dot(own(s, k), metric_rows(s)))

        @pl.loop(0, 2)
        def _(q):
            p = 3 * q + 1
            put_i(s, p, dot_nt(own(s, lax.rem(pairs[p, 0], owned)), own(s, lax.rem(pairs[p, 1], owned))))

    def compute_halo(s):
        @pl.loop(0, 2)
        def _(q):
            p = 3 * q
            put_i(s, p, dot_nt(own(s, lax.rem(pairs[p, 0], owned)), halo_l[s, q]))
            put_i(s, p + 2, dot_nt(own(s, lax.rem(pairs[p + 2, 0], owned)), halo_r[s, q]))

    def compute_halo_c(s):
        @pl.loop(0, 2)
        def _(q):
            put_c(s, owned + q, dot(halo_l[s, q], metric_rows(s)))
            put_c(s, owned + 2 + q, dot(halo_r[s, q], metric_rows(s)))

    for c in range(CHUNKS):
        stage(0, c)

    lanes = min(128, virt)
    vir_rows = jnp.broadcast_to(vir[...], (lanes, virt))
    vir_cols = vir_rows.T

    @pl.loop(0, 6)
    def _(p):
        energy = occ[pairs[p, 0]] + occ[pairs[p, 1]]
        for t in range(virt // lanes):
            span = slice(t * lanes, (t + 1) * lanes)
            recip[p, :, span] = 1.0 / ((energy - vir_cols) - vir[:, span])

    load_m.wait()
    compute_own(0)

    for cu, cd in zip(up_order, down_order):
        send_up[cu].wait_recv()
        if cu < half:
            pass_on[cu].start()
        stage(1, cu)
        send_down[cd].wait_recv()
        if cd >= half:
            pass_on[cd].start()
        stage(2, cd)

    halo_wait(0)
    compute_halo(0)
    compute_halo_c(0)
    for s in (1, 2):
        compute_own(s)
        halo_wait(s)
        compute_halo(s)
        compute_halo_c(s)

    for c in range(half):
        for d in (c, half + c):
            pass_on[d].wait_recv()
            stage(3, d)
    compute_own(3)
    halo_wait(3)
    compute_halo(3)

    term_l = [remote(tsend_l.at[q], trecv_r.at[q], t_send.at[0, q], t_recv.at[0, q], to_l) for q in range(2)]
    term_r = [remote(tsend_r.at[q], trecv_l.at[q], t_send.at[1, q], t_recv.at[1, q], to_r) for q in range(2)]
    for q in range(2):
        for side, p, has, copy, far, near in (
            (0, 3 * q, has_l, term_l[q], tsend_l, trecv_l),
            (1, 3 * q + 2, has_r, term_r[q], tsend_r, trecv_r),
        ):
            value = dot_tn(amp[p], cb[lax.rem(pairs[p, 0], owned)]).astype(BF16)

            @pl.when(has)
            def _():
                far[q] = value
                copy.start()

            @pl.when(jnp.logical_not(has))
            def _():
                near[q] = value

    compute_halo_c(3)

    @pl.loop(0, 2)
    def _(q):
        p = 3 * q
        term[p] = dot(amp[p], cb[owned + q])
        term[p + 1] = dot(amp[p + 1], cb[lax.rem(pairs[p + 1, 1], owned)])
        term[p + 2] = dot(amp[p + 2], cb[owned + 2 + q])
        term[6 + q] = dot_tn(amp[p + 1], cb[lax.rem(pairs[p + 1, 0], owned)])

    step = 16
    targets = [lax.rem(pairs[p, 0], owned) for p in range(6)] + [lax.rem(pairs[3 * q + 1, 1], owned) for q in range(2)]

    @pl.loop(0, virt // step)
    def _(t):
        span = pl.ds(pl.multiple_of(t * step, step), step)
        values = [term[n, span, :] for n in range(8)]
        for k in range(owned):
            total[k, span, :] = sum(jnp.where(target == k, 1.0, 0.0) * v for target, v in zip(targets, values))

    for q in range(2):

        @pl.when(has_r)
        def _():
            term_l[q].wait_recv()

        @pl.when(has_l)
        def _():
            term_r[q].wait_recv()

    arrived = [ids[n] for n in range(4)]

    @pl.loop(0, virt // step)
    def _(t):
        span = pl.ds(pl.multiple_of(t * step, step), step)
        values = [trecv_l[q, span, :].astype(F32) for q in range(2)] + [trecv_r[q, span, :].astype(F32) for q in range(2)]
        for k in range(owned):
            more = sum(jnp.where(target == k, 1.0, 0.0) * v for target, v in zip(arrived, values))
            out[k, span, :] = (total[k, span, :] + more).astype(BF16)

    for c in range(CHUNKS):
        send_up[c].wait_send()
        send_down[c].wait_send()
        pass_on[c].wait_send()

    @pl.when(has_l)
    def _():
        ids_l.wait_send()
        for q in range(2):
            term_l[q].wait_send()
        for s in range(4):
            for c in range(CHUNKS):
                halo_left(s, c).wait_send()

    @pl.when(has_r)
    def _():
        ids_r.wait_send()
        for q in range(2):
            term_r[q].wait_send()
        for s in range(4):
            for c in range(CHUNKS):
                halo_right(s, c).wait_send()


def local(n_orb, b, metric, occ, vir, pairs):
    owned, virt, width = b.shape
    rows = virt // CHUNKS
    vmem = pltpu.VMEM
    dma = pltpu.SemaphoreType.DMA
    scratch = [
        vmem((owned, virt, width), BF16),
        vmem(metric.shape, BF16),
        tuple(tuple(vmem((owned, rows, width), BF16) for _ in range(CHUNKS)) for _ in range(3)),
        vmem((4, 2, virt, width), BF16),
        vmem((4, 2, virt, width), BF16),
        vmem((4, 2, virt, width), BF16),
        vmem((4, 2, virt, width), BF16),
        pltpu.SMEM(pairs.shape, jnp.int32),
        pltpu.SMEM(pairs.shape, jnp.int32),
        pltpu.SMEM((4,), jnp.int32),
        vmem((6, virt, virt), F32),
        vmem((6, virt, virt), F32),
        vmem((owned + 4, virt, width), F32),
        vmem((owned + 4, virt, width), BF16),
        vmem((6, virt, virt), BF16),
        vmem((8, virt, width), F32),
        vmem((owned, virt, width), F32),
        vmem((2, virt, width), BF16),
        vmem((2, virt, width), BF16),
        vmem((2, virt, width), BF16),
        vmem((2, virt, width), BF16),
        dma((2,)),
        dma((2,)),
        dma((2,)),
        dma((3, CHUNKS)),
        dma((3, CHUNKS)),
        dma((2, 4, CHUNKS)),
        dma((2, 4, CHUNKS)),
        dma((2, 2)),
        dma((2, 2)),
    ]
    return pl.pallas_call(
        functools.partial(kernel, n_orb),
        out_shape=jax.ShapeDtypeStruct(b.shape, BF16),
        in_specs=[
            pl.BlockSpec(memory_space=pl.ANY),
            pl.BlockSpec(memory_space=pl.ANY),
            pl.BlockSpec(memory_space=pltpu.SMEM),
            pl.BlockSpec(memory_space=pltpu.VMEM),
            pl.BlockSpec(memory_space=pltpu.SMEM),
        ],
        out_specs=pl.BlockSpec(memory_space=pltpu.VMEM),
        scratch_shapes=scratch,
        compiler_params=pltpu.CompilerParams(
            collective_id=0, has_side_effects=True, vmem_limit_bytes=52 * 2**20
        ),
    )(b, metric, occ, vir.reshape(1, -1), pairs)


def solution(mesh):
    placed = (P("orb", None, "aux"), P(None, "aux"), P(), P(), P("orb", None))
    return jax.shard_map(
        functools.partial(local, mesh.shape["orb"]),
        mesh=mesh,
        in_specs=placed,
        out_specs=P("orb", None, "aux"),
        check_vma=False,
    )
```

time: 222 us -> 75.8 us (0.34)
  waiting for transfers between devices: 92.3 us -> 0 us
  Pallas kernels: 0 us -> 72.4 us
  starting transfers between devices: 42.3 us -> 0 us
  local copies, waits for them, and re-layouts: 43.8 us -> 3.14 us
  matrix products: 23.2 us -> 0 us
  between operations: 13.7 us -> 0.01 us
  other arithmetic: 5.4 us -> 0 us
    pallas_call x0 -> x1, Pallas kernels: none -> 72.4 us  [local(): pl.pallas_call(functools.partial(kernel, n_orb), out_shape=jax.ShapeDtype...]
    all_gather x1 -> x0, waiting for transfers between devices: 60.1 us -> none  [local(): shard_piece = lax.all_gather(density, 'aux', axis=2, tiled=True)]
    ppermute x6 -> x0, starting transfers between devices: 33.3 us -> none  [the longest x4 20.2 us: from_behind(): lax.ppermute(value, axis, [(source, source + steps) for source in range(i...]
    dot_general x9 -> x0, matrix products: 23.2 us -> none  [the longest x2 8.79 us: arrived_terms(): jnp.einsum('nk,nbx->kbx', picker, terms, precision=lax.Precision.HIGHEST)]
    ppermute x6 -> x0, waiting for transfers between devices: 20.4 us -> none  [the longest x1 11.5 us: with_halo(): before = lax.ppermute(last, axis, up)]
    unnamed x28 -> x4, local copies, waits for them, and re-layouts: 18.7 us -> 2.46 us
    gather x4 -> x0, local copies, waits for them, and re-layouts: 13.2 us -> none  [the longest x2 6.12 us: arrived_terms(): blocks = jnp.take(widened, block_ids, axis=0)]
    all_to_all x2 -> x0, waiting for transfers between devices: 11.8 us -> none  [the longest x1 11.8 us: sent_and_summed(): tiles = lax.all_to_all(split_up(array, dim, length), axis, 0, 0, tiled=True)]
  transfers between devices with their start and end apart: 9 -> 0, of which waited for: 4 -> 0; matrix products, arithmetic and copies ran while one was open for 18% -> 0% of each run, Pallas kernels for 0% -> 0%
where the time goes in v1:
time: 75.8 us; the launch traced here: 75.6 us
  Pallas kernels  72.4 us (96%)
  local copies, waits for them, and re-layouts  3.14 us (4%)
    pallas_call x1, Pallas kernels, local(): pl.pallas_call(functools.partial(kernel, n_orb), out_shape=jax.ShapeDtype...  72.4 us
    unnamed x4, local copies, waits for them, and re-layouts  2.46 us

profile of v1, /device:TPU:6, one launch (start us, length us, event | category | flops | bytes accessed | tf_op | source)
XLA Modules:
  0.0 75.6 jit_solution(17501737322112671099)
XLA Ops:
  0.0 0.7 reshape.3.vir
  0.7 0.8 %copy.6.pairs = s32[6,2]{1,0:T(8,128)S(1)} copy(s32[6,2]{0,1:T(2,128)} %param.9) | data formatting | bytes 96 | tf_op args[4]
  1.4 0.0 copy-start
  1.5 0.7 copy-done
  2.1 72.4 %shard_map.55 = bf16[4,384,384]{2,1,0:T(8,128)(2,1)S(1)} custom-call(bf16[4,384,384]{2,1,0:T(8,128)(2,1)} %b_hbm.1, bf16[1536,384]{1,0:T(8,128)(2,1)} %m_hbm.1, f32[512]{0:T(512)S(1)} %copy-done, f32[1,384]{1,0:T(1,128)S(1)} %reshape.3.vir, s32[6,2]{1,0:T(8,128)S(1)} %copy.6.pairs), custom_call_target="tpu_custom_call" | custom-call | tf_op jit(solution)/shard_map/pallas_call | solution.py:412
  74.6 1.0 %copy.8 = bf16[4,384,384]{2,1,0:T(8,128)(2,1)} copy(bf16[4,384,384]{2,1,0:T(8,128)(2,1)S(1)} %shard_map.55) | data formatting | bytes 2359296
Async XLA Ops:
  1.4 0.7 copy-start

commit v2 on v1

--- a/solution.py
+++ b/solution.py
@@ -29,10 +29,13 @@
     n_orb,
     b_hbm,
     m_hbm,
+    occ_hbm,
+    vir_hbm,
+    pairs_hbm,
+    out,
     occ,
     vir,
     pairs,
-    out,
     bown,
     m,
     gathered,
@@ -55,6 +58,7 @@
     trecv_l,
     trecv_r,
     load_sem,
+    entered,
     id_send,
     id_recv,
     y_send,
@@ -77,7 +81,13 @@
 
     load_b = pltpu.make_async_copy(b_hbm, bown, load_sem.at[0])
     load_m = pltpu.make_async_copy(m_hbm, m, load_sem.at[1])
+    load_pairs = pltpu.make_async_copy(pairs_hbm, pairs, load_sem.at[2])
+    load_occ = pltpu.make_async_copy(occ_hbm, occ, load_sem.at[3])
+    load_vir = pltpu.make_async_copy(vir_hbm, vir, load_sem.at[4])
+    load_pairs.start()
     load_b.start()
+    load_occ.start()
+    load_vir.start()
     load_m.start()
 
     barrier = pltpu.get_barrier_semaphore()
@@ -88,11 +98,13 @@
     def _():
         pl.semaphore_signal(barrier, inc=1, device_id=to_l, device_id_type=MESH)
 
+    pl.semaphore_wait(barrier, 2 + has_r.astype(jnp.int32))
+
     @pl.when(has_r)
     def _():
-        pl.semaphore_signal(barrier, inc=1, device_id=to_r, device_id_type=MESH)
-
-    pl.semaphore_wait(barrier, 2 + has_l.astype(jnp.int32) + has_r.astype(jnp.int32))
+        pl.semaphore_signal(entered, inc=1, device_id=to_r, device_id_type=MESH)
+
+    load_pairs.wait()
     load_b.wait()
 
     def remote(src, dst, send, recv, device):
@@ -102,14 +114,6 @@
 
     ids_l = remote(pairs, got_r, id_send.at[0], id_recv.at[0], to_l)
     ids_r = remote(pairs, got_l, id_send.at[1], id_recv.at[1], to_r)
-
-    @pl.when(has_l)
-    def _():
-        ids_l.start()
-
-    @pl.when(has_r)
-    def _():
-        ids_r.start()
 
     def row_span(c):
         return pl.ds(c * rows, rows)
@@ -132,27 +136,36 @@
         send_up[cu].start()
         send_down[cd].start()
 
+    @pl.when(has_r)
+    def _():
+        ids_r.start()
+
     @pl.when(has_l)
     def _():
+        pl.semaphore_wait(entered, 1)
+        ids_l.start()
+
+    @pl.when(has_l)
+    def _():
         ids_r.wait_recv()
         for q in range(2):
-            ids[q] = lax.rem(got_l[3 * q + 2, 1], owned)
+            ids[q] = lax.rem(got_l[1, 3 * q + 2], owned)
 
     @pl.when(jnp.logical_not(has_l))
     def _():
         for q in range(2):
-            ids[q] = lax.rem(pairs[3 * q, 1], owned)
+            ids[q] = lax.rem(pairs[1, 3 * q], owned)
 
     @pl.when(has_r)
     def _():
         ids_l.wait_recv()
         for q in range(2):
-            ids[2 + q] = lax.rem(got_r[3 * q, 1], owned)
+            ids[2 + q] = lax.rem(got_r[1, 3 * q], owned)
 
     @pl.when(jnp.logical_not(has_r))
     def _():
         for q in range(2):
-            ids[2 + q] = lax.rem(pairs[3 * q + 2, 1], owned)
+            ids[2 + q] = lax.rem(pairs[1, 3 * q + 2], owned)
 
     def halo_left(s, c):
         span = row_span(c)
@@ -190,15 +203,21 @@
             for q in range(2):
                 halo_r[s, q, span, :] = pick(s, c, ids[2 + q])
 
+    def wait_right(s):
+        @pl.when(has_r)
+        def _():
+            for c in range(CHUNKS):
+                halo_left(s, c).wait_recv()
+
+    def wait_left(s):
+        @pl.when(has_l)
+        def _():
+            for c in range(CHUNKS):
+                halo_right(s, c).wait_recv()
+
     def halo_wait(s):
-        for c in range(CHUNKS):
-            @pl.when(has_r)
-            def _():
-                halo_left(s, c).wait_recv()
-
-            @pl.when(has_l)
-            def _():
-                halo_right(s, c).wait_recv()
+        wait_right(s)
+        wait_left(s)
 
     def own(s, k):
         return bown[k] if s == 0 else jnp.concatenate([g[k] for g in gathered[s - 1]], axis=0)
@@ -231,14 +250,19 @@
         @pl.loop(0, 2)
         def _(q):
             p = 3 * q + 1
-            put_i(s, p, dot_nt(own(s, lax.rem(pairs[p, 0], owned)), own(s, lax.rem(pairs[p, 1], owned))))
+            put_i(s, p, dot_nt(own(s, lax.rem(pairs[0, p], owned)), own(s, lax.rem(pairs[1, p], owned))))
+
+    def compute_left(s, q):
+        put_i(s, 3 * q, dot_nt(own(s, lax.rem(pairs[0, 3 * q], owned)), halo_l[s, q]))
+
+    def compute_right(s, q):
+        put_i(s, 3 * q + 2, dot_nt(own(s, lax.rem(pairs[0, 3 * q + 2], owned)), halo_r[s, q]))
 
     def compute_halo(s):
         @pl.loop(0, 2)
         def _(q):
-            p = 3 * q
-            put_i(s, p, dot_nt(own(s, lax.rem(pairs[p, 0], owned)), halo_l[s, q]))
-            put_i(s, p + 2, dot_nt(own(s, lax.rem(pairs[p + 2, 0], owned)), halo_r[s, q]))
+            compute_left(s, q)
+            compute_right(s, q)
 
     def compute_halo_c(s):
         @pl.loop(0, 2)
@@ -250,15 +274,18 @@
         stage(0, c)
 
     lanes = min(128, virt)
-    vir_rows = jnp.broadcast_to(vir[...], (lanes, virt))
+    load_occ.wait()
+    load_vir.wait()
+    vir_row = vir[...].reshape(1, virt)
+    vir_rows = jnp.broadcast_to(vir_row, (lanes, virt))
     vir_cols = vir_rows.T
 
     @pl.loop(0, 6)
     def _(p):
-        energy = occ[pairs[p, 0]] + occ[pairs[p, 1]]
+        energy = occ[pairs[0, p]] + occ[pairs[1, p]]
         for t in range(virt // lanes):
             span = slice(t * lanes, (t + 1) * lanes)
-            recip[p, :, span] = 1.0 / ((energy - vir_cols) - vir[:, span])
+            recip[p, :, span] = 1.0 / ((energy - vir_cols) - vir_row[:, span])
 
     load_m.wait()
     compute_own(0)
@@ -287,22 +314,22 @@
             pass_on[d].wait_recv()
             stage(3, d)
     compute_own(3)
-    halo_wait(3)
-    compute_halo(3)
-
     term_l = [remote(tsend_l.at[q], trecv_r.at[q], t_send.at[0, q], t_recv.at[0, q], to_l) for q in range(2)]
     term_r = [remote(tsend_r.at[q], trecv_l.at[q], t_send.at[1, q], t_recv.at[1, q], to_r) for q in range(2)]
-    for q in range(2):
-        for side, p, has, copy, far, near in (
-            (0, 3 * q, has_l, term_l[q], tsend_l, trecv_l),
-            (1, 3 * q + 2, has_r, term_r[q], tsend_r, trecv_r),
-        ):
-            value = dot_tn(amp[p], cb[lax.rem(pairs[p, 0], owned)]).astype(BF16)
+    for ready, work, slot, has, copies, far, near in (
+        (wait_right, compute_right, 2, has_r, term_r, tsend_r, trecv_r),
+        (wait_left, compute_left, 0, has_l, term_l, tsend_l, trecv_l),
+    ):
+        ready(3)
+        for q in range(2):
+            p = 3 * q + slot
+            work(3, q)
+            value = dot_tn(amp[p], cb[lax.rem(pairs[0, p], owned)]).astype(BF16)
 
             @pl.when(has)
             def _():
                 far[q] = value
-                copy.start()
+                copies[q].start()
 
             @pl.when(jnp.logical_not(has))
             def _():
@@ -314,12 +341,12 @@
     def _(q):
         p = 3 * q
         term[p] = dot(amp[p], cb[owned + q])
-        term[p + 1] = dot(amp[p + 1], cb[lax.rem(pairs[p + 1, 1], owned)])
+        term[p + 1] = dot(amp[p + 1], cb[lax.rem(pairs[1, p + 1], owned)])
         term[p + 2] = dot(amp[p + 2], cb[owned + 2 + q])
-        term[6 + q] = dot_tn(amp[p + 1], cb[lax.rem(pairs[p + 1, 0], owned)])
+        term[6 + q] = dot_tn(amp[p + 1], cb[lax.rem(pairs[0, p + 1], owned)])
 
     step = 16
-    targets = [lax.rem(pairs[p, 0], owned) for p in range(6)] + [lax.rem(pairs[3 * q + 1, 1], owned) for q in range(2)]
+    targets = [lax.rem(pairs[0, p], owned) for p in range(6)] + [lax.rem(pairs[1, 3 * q + 1], owned) for q in range(2)]
 
     @pl.loop(0, virt // step)
     def _(t):
@@ -373,11 +400,15 @@
 
 
 def local(n_orb, b, metric, occ, vir, pairs):
+    pairs_t = pairs.T
     owned, virt, width = b.shape
     rows = virt // CHUNKS
     vmem = pltpu.VMEM
     dma = pltpu.SemaphoreType.DMA
     scratch = [
+        pltpu.SMEM(occ.shape, F32),
+        vmem(vir.shape, F32),
+        pltpu.SMEM(pairs_t.shape, jnp.int32),
         vmem((owned, virt, width), BF16),
         vmem(metric.shape, BF16),
         tuple(tuple(vmem((owned, rows, width), BF16) for _ in range(CHUNKS)) for _ in range(3)),
@@ -385,8 +416,8 @@
         vmem((4, 2, virt, width), BF16),
         vmem((4, 2, virt, width), BF16),
         vmem((4, 2, virt, width), BF16),
-        pltpu.SMEM(pairs.shape, jnp.int32),
-        pltpu.SMEM(pairs.shape, jnp.int32),
+        pltpu.SMEM(pairs_t.shape, jnp.int32),
+        pltpu.SMEM(pairs_t.shape, jnp.int32),
         pltpu.SMEM((4,), jnp.int32),
         vmem((6, virt, virt), F32),
         vmem((6, virt, virt), F32),
@@ -399,7 +430,8 @@
         vmem((2, virt, width), BF16),
         vmem((2, virt, width), BF16),
         vmem((2, virt, width), BF16),
-        dma((2,)),
+        dma((5,)),
+        pltpu.SemaphoreType.REGULAR,
         dma((2,)),
         dma((2,)),
         dma((3, CHUNKS)),
@@ -412,19 +444,13 @@
     return pl.pallas_call(
         functools.partial(kernel, n_orb),
         out_shape=jax.ShapeDtypeStruct(b.shape, BF16),
-        in_specs=[
-            pl.BlockSpec(memory_space=pl.ANY),
-            pl.BlockSpec(memory_space=pl.ANY),
-            pl.BlockSpec(memory_space=pltpu.SMEM),
-            pl.BlockSpec(memory_space=pltpu.VMEM),
-            pl.BlockSpec(memory_space=pltpu.SMEM),
-        ],
+        in_specs=[pl.BlockSpec(memory_space=pltpu.HBM)] * 5,
         out_specs=pl.BlockSpec(memory_space=pltpu.VMEM),
         scratch_shapes=scratch,
         compiler_params=pltpu.CompilerParams(
             collective_id=0, has_side_effects=True, vmem_limit_bytes=52 * 2**20
         ),
-    )(b, metric, occ, vir.reshape(1, -1), pairs)
+    )(b, metric, occ, vir, pairs_t)
 
 
 def solution(mesh):

time: 75.8 us -> 73.8 us (0.974)
  Pallas kernels: 72.4 us -> 70.6 us
    pallas_call x1, Pallas kernels: 72.4 us -> 70.6 us  [local(): pl.pallas_call(functools.partial(kernel, n_orb), out_shape=jax.ShapeDtype...]
    unnamed x4 -> x7, local copies, waits for them, and re-layouts: 2.46 us -> 3.06 us
where the time goes in v2:
time: 73.8 us; the launch traced here: 73.6 us
  Pallas kernels  70.6 us (96%)
  local copies, waits for them, and re-layouts  3.06 us (4%)
    pallas_call x1, Pallas kernels, local(): pl.pallas_call(functools.partial(kernel, n_orb), out_shape=jax.ShapeDtype...  70.6 us
    unnamed x7, local copies, waits for them, and re-layouts  3.06 us

profile of v2, /device:TPU:6, one launch (start us, length us, event | category | flops | bytes accessed | tf_op | source)
XLA Modules:
  0.0 73.6 jit_solution(9440858814123452034)
XLA Ops:
  0.0 0.0 copy-start
  0.0 0.7 copy-done
  0.7 0.0 copy-start.1
  0.7 0.7 copy-done.1
  1.4 0.0 copy-start.2
  1.4 0.7 copy-done.2
  2.0 70.6 %shard_map.55 = bf16[4,384,384]{2,1,0:T(8,128)(2,1)S(1)} custom-call(bf16[4,384,384]{2,1,0:T(8,128)(2,1)} %b_hbm.1, bf16[1536,384]{1,0:T(8,128)(2,1)} %m_hbm.1, f32[512]{0:T(512)S(1)} %copy-done, f32[384]{0:T(512)S(1)} %copy-done.1, s32[2,6]{1,0:T(2,128)S(1)} %bitcast.1), custom_call_target="tpu_custom_call" | custom-call | tf_op jit(solution)/shard_map/pallas_call | solution.py:444
  72.6 1.0 %copy.7 = bf16[4,384,384]{2,1,0:T(8,128)(2,1)} copy(bf16[4,384,384]{2,1,0:T(8,128)(2,1)S(1)} %shard_map.55) | data formatting | bytes 2359296
Async XLA Ops:
  0.0 0.7 copy-start
  0.7 0.7 copy-start.1
  1.4 0.7 copy-start.2

commit v3 on v2

--- a/solution.py
+++ b/solution.py
@@ -215,10 +215,6 @@
             for c in range(CHUNKS):
                 halo_right(s, c).wait_recv()
 
-    def halo_wait(s):
-        wait_right(s)
-        wait_left(s)
-
     def own(s, k):
         return bown[k] if s == 0 else jnp.concatenate([g[k] for g in gathered[s - 1]], axis=0)
 
@@ -258,17 +254,23 @@
     def compute_right(s, q):
         put_i(s, 3 * q + 2, dot_nt(own(s, lax.rem(pairs[0, 3 * q + 2], owned)), halo_r[s, q]))
 
-    def compute_halo(s):
+    def compute_left_c(s, q):
+        put_c(s, owned + q, dot(halo_l[s, q], metric_rows(s)))
+
+    def compute_right_c(s, q):
+        put_c(s, owned + 2 + q, dot(halo_r[s, q], metric_rows(s)))
+
+    def both_left(s):
         @pl.loop(0, 2)
         def _(q):
             compute_left(s, q)
-            compute_right(s, q)
-
-    def compute_halo_c(s):
+            compute_left_c(s, q)
+
+    def both_right(s):
         @pl.loop(0, 2)
         def _(q):
-            put_c(s, owned + q, dot(halo_l[s, q], metric_rows(s)))
-            put_c(s, owned + 2 + q, dot(halo_r[s, q], metric_rows(s)))
+            compute_right(s, q)
+            compute_right_c(s, q)
 
     for c in range(CHUNKS):
         stage(0, c)
@@ -300,19 +302,24 @@
             pass_on[cd].start()
         stage(2, cd)
 
-    halo_wait(0)
-    compute_halo(0)
-    compute_halo_c(0)
-    for s in (1, 2):
-        compute_own(s)
-        halo_wait(s)
-        compute_halo(s)
-        compute_halo_c(s)
-
-    for c in range(half):
+    def stage_passed(c):
         for d in (c, half + c):
             pass_on[d].wait_recv()
             stage(3, d)
+
+    compute_own(1)
+    compute_own(2)
+    for s in range(3):
+        wait_right(s)
+        both_right(s)
+    wait_left(0)
+    both_left(0)
+    for c in range(half - 1):
+        stage_passed(c)
+    for s in (1, 2):
+        wait_left(s)
+        both_left(s)
+    stage_passed(half - 1)
     compute_own(3)
     term_l = [remote(tsend_l.at[q], trecv_r.at[q], t_send.at[0, q], t_recv.at[0, q], to_l) for q in range(2)]
     term_r = [remote(tsend_r.at[q], trecv_l.at[q], t_send.at[1, q], t_recv.at[1, q], to_r) for q in range(2)]
@@ -335,10 +342,10 @@
             def _():
                 near[q] = value
 
-    compute_halo_c(3)
-
     @pl.loop(0, 2)
     def _(q):
+        compute_left_c(3, q)
+        compute_right_c(3, q)
         p = 3 * q
         term[p] = dot(amp[p], cb[owned + q])
         term[p + 1] = dot(amp[p + 1], cb[lax.rem(pairs[1, p + 1], owned)])

time: 73.8 us -> 69.1 us (0.936)
  Pallas kernels: 70.6 us -> 65.8 us
    pallas_call x1, Pallas kernels: 70.6 us -> 65.8 us  [local(): pl.pallas_call(functools.partial(kernel, n_orb), out_shape=jax.ShapeDtype...]
where the time goes in v3:
time: 69.1 us; the launch traced here: 68.9 us
  Pallas kernels  65.8 us (95%)
  local copies, waits for them, and re-layouts  3.06 us (4%)
    pallas_call x1, Pallas kernels, local(): pl.pallas_call(functools.partial(kernel, n_orb), out_shape=jax.ShapeDtype...  65.8 us
    unnamed x7, local copies, waits for them, and re-layouts  3.06 us

profile of v3, /device:TPU:6, one launch (start us, length us, event | category | flops | bytes accessed | tf_op | source)
XLA Modules:
  0.0 68.9 jit_solution(14991703048667996241)
XLA Ops:
  0.0 0.0 copy-start
  0.0 0.7 copy-done
  0.7 0.0 copy-start.1
  0.7 0.7 copy-done.1
  1.4 0.0 copy-start.2
  1.4 0.7 copy-done.2
  2.0 65.8 %shard_map.55 = bf16[4,384,384]{2,1,0:T(8,128)(2,1)S(1)} custom-call(bf16[4,384,384]{2,1,0:T(8,128)(2,1)} %b_hbm.1, bf16[1536,384]{1,0:T(8,128)(2,1)} %m_hbm.1, f32[512]{0:T(512)S(1)} %copy-done, f32[384]{0:T(512)S(1)} %copy-done.1, s32[2,6]{1,0:T(2,128)S(1)} %bitcast.1), custom_call_target="tpu_custom_call" | custom-call | tf_op jit(solution)/shard_map/pallas_call | solution.py:451
  67.9 1.0 %copy.7 = bf16[4,384,384]{2,1,0:T(8,128)(2,1)} copy(bf16[4,384,384]{2,1,0:T(8,128)(2,1)S(1)} %shard_map.55) | data formatting | bytes 2359296
Async XLA Ops:
  0.0 0.7 copy-start
  0.7 0.7 copy-start.1
  1.4 0.7 copy-start.2

commit v4 on v3

v4 whole, which is shorter than its diff:
```python
import functools

import jax
import jax.numpy as jnp
from jax import lax
from jax.experimental import pallas as pl
from jax.experimental.pallas import tpu as pltpu
from jax.sharding import PartitionSpec as P

MESH = pl.DeviceIdType.MESH
F32 = jnp.float32
BF16 = jnp.bfloat16
PARTS = (96, 64, 32)
LINE = 32


def dot(a, b):
    return lax.dot_general(a, b, (((1,), (0,)), ((), ())), preferred_element_type=F32)


def dot_nt(a, b):
    return lax.dot_general(a, b, (((1,), (1,)), ((), ())), preferred_element_type=F32)


def dot_tn(a, b):
    return lax.dot_general(a, b, (((0,), (0,)), ((), ())), preferred_element_type=F32)


def chunk_rows(virt):
    sizes = [part * virt // (2 * sum(PARTS)) for part in PARTS] * 2
    return sizes, [sum(sizes[:c]) for c in range(len(sizes))]


def kernel(
    n_orb,
    b_hbm,
    m_hbm,
    occ_hbm,
    vir_hbm,
    pairs_hbm,
    out,
    occ,
    vir,
    pairs,
    bown,
    m,
    gathered,
    halo_l,
    halo_r,
    stage_l,
    stage_r,
    got_l,
    got_r,
    ids,
    acc_i,
    recip,
    acc_c,
    cb,
    amp,
    term,
    total,
    tsend_l,
    tsend_r,
    trecv_l,
    trecv_r,
    load_sem,
    entered,
    id_send,
    id_recv,
    y_send,
    y_recv,
    z_send,
    z_recv,
    t_send,
    t_recv,
):
    owned, virt, width = bown.shape
    sizes, starts = chunk_rows(virt)
    count = len(sizes)
    half = count // 2
    o = lax.axis_index("orb")
    y = lax.axis_index("aux")
    has_l = o > 0
    has_r = o < n_orb - 1
    up, down = lax.rem(y + 1, 4), lax.rem(y + 3, 4)
    to_up, to_down = (o, up), (o, down)
    to_l, to_r = (o - 1, y), (o + 1, y)

    load_b = pltpu.make_async_copy(b_hbm, bown, load_sem.at[0])
    sources = (y, down, up, lax.rem(y + 2, 4))
    load_m = [
        pltpu.make_async_copy(
            m_hbm.at[pl.ds(pl.multiple_of(source * width, width), width), :],
            m.at[pl.ds(s * width, width), :],
            load_sem.at[4 + s],
        )
        for s, source in enumerate(sources)
    ]
    load_pairs = pltpu.make_async_copy(pairs_hbm, pairs, load_sem.at[1])
    load_occ = pltpu.make_async_copy(occ_hbm, occ, load_sem.at[2])
    load_vir = pltpu.make_async_copy(vir_hbm, vir, load_sem.at[3])
    load_pairs.start()
    load_b.start()
    load_occ.start()
    load_vir.start()
    for piece in load_m:
        piece.start()

    barrier = pltpu.get_barrier_semaphore()
    pl.semaphore_signal(barrier, inc=1, device_id=to_up, device_id_type=MESH)
    pl.semaphore_signal(barrier, inc=1, device_id=to_down, device_id_type=MESH)

    @pl.when(has_l)
    def _():
        pl.semaphore_signal(barrier, inc=1, device_id=to_l, device_id_type=MESH)

    pl.semaphore_wait(barrier, 2 + has_r.astype(jnp.int32))

    @pl.when(has_r)
    def _():
        pl.semaphore_signal(entered, inc=1, device_id=to_r, device_id_type=MESH)

    load_pairs.wait()
    load_b.wait()

    def remote(src, dst, send, recv, device):
        return pltpu.make_async_remote_copy(
            src_ref=src, dst_ref=dst, send_sem=send, recv_sem=recv, device_id=device, device_id_type=MESH
        )

    ids_l = remote(pairs, got_r, id_send.at[0], id_recv.at[0], to_l)
    ids_r = remote(pairs, got_l, id_send.at[1], id_recv.at[1], to_r)

    def row_span(c):
        return pl.ds(starts[c], sizes[c])

    send_up = [
        remote(bown.at[:, row_span(c)], gathered[0][c], y_send.at[0, c], y_recv.at[0, c], to_up) for c in range(count)
    ]
    send_down = [
        remote(bown.at[:, row_span(c)], gathered[1][c], y_send.at[1, c], y_recv.at[1, c], to_down) for c in range(count)
    ]
    pass_on = [
        remote(gathered[0][c], gathered[2][c], y_send.at[2, c], y_recv.at[2, c], to_up)
        if c < half
        else remote(gathered[1][c], gathered[2][c], y_send.at[2, c], y_recv.at[2, c], to_down)
        for c in range(count)
    ]
    up_order = list(range(count))
    down_order = up_order[half:] + up_order[:half]
    for cu, cd in zip(up_order, down_order):
        send_up[cu].start()
        send_down[cd].start()

    @pl.when(has_r)
    def _():
        ids_r.start()

    @pl.when(has_l)
    def _():
        pl.semaphore_wait(entered, 1)
        ids_l.start()

    @pl.when(has_l)
    def _():
        ids_r.wait_recv()
        for q in range(2):
            ids[q] = lax.rem(got_l[1, 3 * q + 2], owned)

    @pl.when(jnp.logical_not(has_l))
    def _():
        for q in range(2):
            ids[q] = lax.rem(pairs[1, 3 * q], owned)

    @pl.when(has_r)
    def _():
        ids_l.wait_recv()
        for q in range(2):
            ids[2 + q] = lax.rem(got_r[1, 3 * q], owned)

    @pl.when(jnp.logical_not(has_r))
    def _():
        for q in range(2):
            ids[2 + q] = lax.rem(pairs[1, 3 * q + 2], owned)

    def lanes_of(s):
        return pl.ds(s * width, width)

    def halo_left(s, c):
        span = row_span(c)
        return remote(stage_l.at[s, :, span], halo_r.at[:, span, lanes_of(s)], z_send.at[0, s, c], z_recv.at[0, s, c], to_l)

    def halo_right(s, c):
        span = row_span(c)
        return remote(stage_r.at[s, :, span], halo_l.at[:, span, lanes_of(s)], z_send.at[1, s, c], z_recv.at[1, s, c], to_r)

    def pick(s, c, k):
        return bown[k, row_span(c), :] if s == 0 else gathered[s - 1][c][k]

    def stage(s, c):
        span = row_span(c)

        @pl.when(has_l)
        def _():
            for q in range(2):
                stage_l[s, q, span, :] = pick(s, c, ids[q])
            halo_left(s, c).start()

        @pl.when(jnp.logical_not(has_l))
        def _():
            for q in range(2):
                halo_l[q, span, lanes_of(s)] = pick(s, c, ids[q])

        @pl.when(has_r)
        def _():
            for q in range(2):
                stage_r[s, q, span, :] = pick(s, c, ids[2 + q])
            halo_right(s, c).start()

        @pl.when(jnp.logical_not(has_r))
        def _():
            for q in range(2):
                halo_r[q, span, lanes_of(s)] = pick(s, c, ids[2 + q])

    def wait_right(s):
        @pl.when(has_r)
        def _():
            for c in range(count):
                halo_left(s, c).wait_recv()

    def wait_left(s):
        @pl.when(has_l)
        def _():
            for c in range(count):
                halo_right(s, c).wait_recv()

    def own(lo, hi, k):
        parts = [
            bown[k] if s == 0 else jnp.concatenate([g[k] for g in gathered[s - 1]], axis=0) for s in range(lo, hi)
        ]
        return parts[0] if len(parts) == 1 else jnp.concatenate(parts, axis=1)

    def metric_rows(lo, hi):
        return m[pl.ds(lo * width, (hi - lo) * width), :]

    def halo(ref, lo, hi, q):
        return ref[q, :, pl.ds(lo * width, (hi - lo) * width)]

    def put_c(lo, hi, slot, value):
        if hi == 4:
            cb[slot] = (acc_c[slot] + value).astype(BF16)
        elif lo == 0:
            acc_c[slot] = value
        else:
            acc_c[slot] += value

    def put_i(lo, hi, slot, value):
        if hi == 4:
            amp[slot] = ((acc_i[slot] + value) * recip[slot]).astype(BF16)
        elif lo == 0:
            acc_i[slot] = value
        else:
            acc_i[slot] += value

    def compute_own_c(lo, hi):
        @pl.loop(0, owned)
        def _(k):
            put_c(lo, hi, k, dot(own(lo, hi, k), metric_rows(lo, hi)))

    def compute_own_i(lo, hi):
        @pl.loop(0, 2)
        def _(q):
            p = 3 * q + 1
            first = own(lo, hi, lax.rem(pairs[0, p], owned))
            put_i(lo, hi, p, dot_nt(first, own(lo, hi, lax.rem(pairs[1, p], owned))))

    def compute_left(lo, hi, q):
        first = own(lo, hi, lax.rem(pairs[0, 3 * q], owned))
        put_i(lo, hi, 3 * q, dot_nt(first, halo(halo_l, lo, hi, q)))

    def compute_right(lo, hi, q):
        first = own(lo, hi, lax.rem(pairs[0, 3 * q + 2], owned))
        put_i(lo, hi, 3 * q + 2, dot_nt(first, halo(halo_r, lo, hi, q)))

    def compute_left_c(lo, hi, q):
        put_c(lo, hi, owned + q, dot(halo(halo_l, lo, hi, q), metric_rows(lo, hi)))

    def compute_right_c(lo, hi, q):
        put_c(lo, hi, owned + 2 + q, dot(halo(halo_r, lo, hi, q), metric_rows(lo, hi)))

    def both_left(lo, hi):
        @pl.loop(0, 2)
        def _(q):
            compute_left(lo, hi, q)
            compute_left_c(lo, hi, q)

    def both_right(lo, hi):
        @pl.loop(0, 2)
        def _(q):
            compute_right(lo, hi, q)
            compute_right_c(lo, hi, q)

    for c in range(count):
        stage(0, c)

    lanes = min(128, virt)
    load_occ.wait()
    load_vir.wait()
    vir_row = vir[...].reshape(1, virt)
    vir_rows = jnp.broadcast_to(vir_row, (lanes, virt))
    vir_cols = vir_rows.T

    @pl.loop(0, 6)
    def _(p):
        energy = occ[pairs[0, p]] + occ[pairs[1, p]]
        for t in range(virt // lanes):
            span = slice(t * lanes, (t + 1) * lanes)
            recip[p, :, span] = 1.0 / ((energy - vir_cols) - vir_row[:, span])

    for piece in load_m:
        piece.wait()
    compute_own_c(0, 1)
    compute_own_i(0, 1)

    for cu, cd in zip(up_order, down_order):
        send_up[cu].wait_recv()
        if cu < half:
            pass_on[cu].start()
        stage(1, cu)
        send_down[cd].wait_recv()
        if cd >= half:
            pass_on[cd].start()
        stage(2, cd)

    def stage_passed(c):
        for d in (c, half + c):
            pass_on[d].wait_recv()
            stage(3, d)

    compute_own_c(1, 3)
    compute_own_i(1, 3)
    for s in range(3):
        wait_right(s)
    both_right(0, 3)
    for c in range(half - 1):
        stage_passed(c)
    for s in range(3):
        wait_left(s)
    both_left(0, 3)
    stage_passed(half - 1)

    term_l = [remote(tsend_l.at[q], trecv_r.at[q], t_send.at[0, q], t_recv.at[0, q], to_l) for q in range(2)]
    term_r = [remote(tsend_r.at[q], trecv_l.at[q], t_send.at[1, q], t_recv.at[1, q], to_r) for q in range(2)]
    sides = (
        (wait_left, compute_left, 0, has_l, term_l, tsend_l, trecv_l),
        (wait_right, compute_right, 2, has_r, term_r, tsend_r, trecv_r),
    )

    def give_terms(side):
        ready, work, slot, has, copies, far, near = sides[side]
        ready(3)
        for q in range(2):
            p = 3 * q + slot
            work(3, 4, q)
            value = dot_tn(amp[p], cb[lax.rem(pairs[0, p], owned)]).astype(BF16)

            @pl.when(has)
            def _():
                far[q] = value
                copies[q].start()

            @pl.when(jnp.logical_not(has))
            def _():
                near[q] = value

    def keep_terms(side):
        @pl.loop(0, 2)
        def _(q):
            (compute_left_c, compute_right_c)[side](3, 4, q)
            p = 3 * q + 2 * side
            term[p] = dot(amp[p], cb[owned + 2 * side + q])

    step = 16

    def gather_terms(terms, start, finish):
        @pl.loop(0, virt // step)
        def _(t):
            span = pl.ds(pl.multiple_of(t * step, step), step)
            values = [ref[n, span, :].astype(F32) for ref, n, _ in terms]
            for k in range(owned):
                more = sum(jnp.where(target == k, 1.0, 0.0) * v for (_, _, target), v in zip(terms, values))
                if not start:
                    more += total[k, span, :]
                if finish:
                    out[k, span, :] = more.astype(BF16)
                else:
                    total[k, span, :] = more

    early_right = jnp.logical_and(has_r, lax.rem(o, LINE) == LINE - 1)
    late_left = jnp.logical_and(has_l, lax.rem(o, LINE) == 0)

    compute_own_c(3, 4)

    @pl.when(early_right)
    def _():
        give_terms(1)

    compute_own_i(3, 4)

    @pl.when(jnp.logical_not(early_right))
    def _():
        give_terms(1)

    left_of = [lax.rem(pairs[0, p], owned) for p in range(6)]

    def own_terms():
        @pl.loop(0, 2)
        def _(q):
            p = 3 * q + 1
            term[p] = dot(amp[p], cb[lax.rem(pairs[1, p], owned)])
            term[6 + q] = dot_tn(amp[p], cb[lax.rem(pairs[0, p], owned)])

        gather_terms(
            [(term, 1, left_of[1]), (term, 4, left_of[4])]
            + [(term, 6 + q, lax.rem(pairs[1, 3 * q + 1], owned)) for q in range(2)],
            True,
            False,
        )

    @pl.when(late_left)
    def _():
        own_terms()
        keep_terms(1)

    give_terms(0)

    @pl.when(jnp.logical_not(late_left))
    def _():
        own_terms()
        keep_terms(1)

    keep_terms(0)

    for q in range(2):

        @pl.when(has_r)
        def _():
            term_l[q].wait_recv()

        @pl.when(has_l)
        def _():
            term_r[q].wait_recv()

        kept = [(term, p, left_of[p]) for p in (0, 2, 3, 5)] if q == 0 else []
        gather_terms(kept + [(trecv_l, q, ids[q]), (trecv_r, q, ids[2 + q])], False, q == 1)

    for c in range(count):
        send_up[c].wait_send()
        send_down[c].wait_send()
        pass_on[c].wait_send()

    @pl.when(has_l)
    def _():
        ids_l.wait_send()
        for q in range(2):
            term_l[q].wait_send()
        for s in range(4):
            for c in range(count):
                halo_left(s, c).wait_send()

    @pl.when(has_r)
    def _():
        ids_r.wait_send()
        for q in range(2):
            term_r[q].wait_send()
        for s in range(4):
            for c in range(count):
                halo_right(s, c).wait_send()


def local(n_orb, b, metric, occ, vir, pairs):
    pairs_t = pairs.T
    owned, virt, width = b.shape
    sizes, _ = chunk_rows(virt)
    count = len(sizes)
    vmem = pltpu.VMEM
    dma = pltpu.SemaphoreType.DMA
    scratch = [
        pltpu.SMEM(occ.shape, F32),
        vmem(vir.shape, F32),
        pltpu.SMEM(pairs_t.shape, jnp.int32),
        vmem((owned, virt, width), BF16),
        vmem(metric.shape, BF16),
        tuple(tuple(vmem((owned, rows, width), BF16) for rows in sizes) for _ in range(3)),
        vmem((2, virt, 4 * width), BF16),
        vmem((2, virt, 4 * width), BF16),
        vmem((4, 2, virt, width), BF16),
        vmem((4, 2, virt, width), BF16),
        pltpu.SMEM(pairs_t.shape, jnp.int32),
        pltpu.SMEM(pairs_t.shape, jnp.int32),
        pltpu.SMEM((4,), jnp.int32),
        vmem((6, virt, virt), F32),
        vmem((6, virt, virt), F32),
        vmem((owned + 4, virt, width), F32),
        vmem((owned + 4, virt, width), BF16),
        vmem((6, virt, virt), BF16),
        vmem((8, virt, width), F32),
        vmem((owned, virt, width), F32),
        vmem((2, virt, width), BF16),
        vmem((2, virt, width), BF16),
        vmem((2, virt, width), BF16),
        vmem((2, virt, width), BF16),
        dma((8,)),
        pltpu.SemaphoreType.REGULAR,
        dma((2,)),
        dma((2,)),
        dma((3, count)),
        dma((3, count)),
        dma((2, 4, count)),
        dma((2, 4, count)),
        dma((2, 2)),
        dma((2, 2)),
    ]
    return pl.pallas_call(
        functools.partial(kernel, n_orb),
        out_shape=jax.ShapeDtypeStruct(b.shape, BF16),
        in_specs=[pl.BlockSpec(memory_space=pltpu.HBM)] * 5,
        out_specs=pl.BlockSpec(memory_space=pltpu.VMEM),
        scratch_shapes=scratch,
        compiler_params=pltpu.CompilerParams(
            collective_id=0, has_side_effects=True, vmem_limit_bytes=52 * 2**20
        ),
    )(b, metric, *(pltpu.with_memory_space_constraint(a, pltpu.HBM) for a in (occ, vir, pairs_t)))


def solution(mesh):
    placed = (P("orb", None, "aux"), P(None, "aux"), P(), P(), P("orb", None))
    return jax.shard_map(
        functools.partial(local, mesh.shape["orb"]),
        mesh=mesh,
        in_specs=placed,
        out_specs=P("orb", None, "aux"),
        check_vma=False,
    )
```

time: 69.1 us -> 65.6 us (0.949)
  local copies, waits for them, and re-layouts: 3.06 us -> 1.02 us
  Pallas kernels: 65.8 us -> 64.4 us
    unnamed x7 -> x1, local copies, waits for them, and re-layouts: 3.06 us -> 1.02 us
    pallas_call x1, Pallas kernels: 65.8 us -> 64.4 us  [local(): pl.pallas_call(functools.partial(kernel, n_orb), out_shape=jax.ShapeDtype...]
where the time goes in v4:
time: 65.6 us; the launch traced here: 65.5 us
  Pallas kernels  64.4 us (98%)
  local copies, waits for them, and re-layouts  1.02 us (2%)
    pallas_call x1, Pallas kernels, local(): pl.pallas_call(functools.partial(kernel, n_orb), out_shape=jax.ShapeDtype...  64.4 us

profile of v4, /device:TPU:6, one launch (start us, length us, event | category | flops | bytes accessed | tf_op | source)
XLA Modules:
  0.0 65.5 jit_solution(2155740058243435137)
XLA Ops:
  0.0 64.4 %shard_map.55 = bf16[4,384,384]{2,1,0:T(8,128)(2,1)S(1)} custom-call(bf16[4,384,384]{2,1,0:T(8,128)(2,1)} %b_hbm.1, bf16[1536,384]{1,0:T(8,128)(2,1)} %m_hbm.1, f32[512]{0:T(512)} %occ_hbm.1, f32[384]{0:T(512)} %vir_hbm.1, s32[2,6]{1,0:T(2,128)} %bitcast.1), custom_call_target="tpu_custom_call" | custom-call | tf_op jit(solution)/shard_map/pallas_call | solution.py:524
  64.4 1.0 %copy.7 = bf16[4,384,384]{2,1,0:T(8,128)(2,1)} copy(bf16[4,384,384]{2,1,0:T(8,128)(2,1)S(1)} %shard_map.55) | data formatting | bytes 2359296

commit v5 on v4

--- a/solution.py
+++ b/solution.py
@@ -148,9 +148,17 @@
     ]
     up_order = list(range(count))
     down_order = up_order[half:] + up_order[:half]
-    for cu, cd in zip(up_order, down_order):
-        send_up[cu].start()
-        send_down[cd].start()
+
+    def start_ring():
+        for cu, cd in zip(up_order, down_order):
+            send_up[cu].start()
+            send_down[cd].start()
+
+    yields = lax.rem(o, LINE) == LINE - 2
+
+    @pl.when(jnp.logical_not(yields))
+    def _():
+        start_ring()
 
     @pl.when(has_r)
     def _():
@@ -321,6 +329,10 @@
         piece.wait()
     compute_own_c(0, 1)
     compute_own_i(0, 1)
+
+    @pl.when(yields)
+    def _():
+        start_ring()
 
     for cu, cd in zip(up_order, down_order):
         send_up[cu].wait_recv()

time: 65.6 us -> 63.8 us (0.973); the launches traced: 65.5 us -> 62.7 us
  Pallas kernels: 64.4 us -> 61.6 us
    pallas_call x1, Pallas kernels: 64.4 us -> 61.6 us  [local(): pl.pallas_call(functools.partial(kernel, n_orb), out_shape=jax.ShapeDtype...]
where the time goes in v5:
time: 63.8 us; the launch traced here: 62.7 us
  Pallas kernels  61.6 us (97%)
  local copies, waits for them, and re-layouts  1.02 us (2%)
    pallas_call x1, Pallas kernels, local(): pl.pallas_call(functools.partial(kernel, n_orb), out_shape=jax.ShapeDtype...  61.6 us

profile of v5, /device:TPU:6, one launch (start us, length us, event | category | flops | bytes accessed | tf_op | source)
XLA Modules:
  0.0 62.7 jit_solution(10899945121509934201)
XLA Ops:
  0.0 61.6 %shard_map.55 = bf16[4,384,384]{2,1,0:T(8,128)(2,1)S(1)} custom-call(bf16[4,384,384]{2,1,0:T(8,128)(2,1)} %b_hbm.1, bf16[1536,384]{1,0:T(8,128)(2,1)} %m_hbm.1, f32[512]{0:T(512)} %occ_hbm.1, f32[384]{0:T(512)} %vir_hbm.1, s32[2,6]{1,0:T(2,128)} %bitcast.1), custom_call_target="tpu_custom_call" | custom-call | tf_op jit(solution)/shard_map/pallas_call | solution.py:536
  61.7 1.0 %copy.7 = bf16[4,384,384]{2,1,0:T(8,128)(2,1)} copy(bf16[4,384,384]{2,1,0:T(8,128)(2,1)S(1)} %shard_map.55) | data formatting | bytes 2359296

commit v6 on v5

--- a/solution.py
+++ b/solution.py
@@ -154,7 +154,8 @@
             send_up[cu].start()
             send_down[cd].start()
 
-    yields = lax.rem(o, LINE) == LINE - 2
+    place = lax.rem(o, LINE)
+    yields = jnp.logical_or(place == LINE - 2, jnp.logical_or(place == 9, place == 17))
 
     @pl.when(jnp.logical_not(yields))
     def _():
@@ -328,11 +329,12 @@
     for piece in load_m:
         piece.wait()
     compute_own_c(0, 1)
+
+    @pl.when(yields)
+    def _():
+        start_ring()
+
     compute_own_i(0, 1)
-
-    @pl.when(yields)
-    def _():
-        start_ring()
 
     for cu, cd in zip(up_order, down_order):
         send_up[cu].wait_recv()

time: 63.8 us -> 64.1 us (level)
  the two profiles are of different devices: /device:TPU:6 before, /device:TPU:135 now
where the time goes in v6:
time: 64.1 us; the launch traced here: 64 us
  Pallas kernels  63 us (98%)
  local copies, waits for them, and re-layouts  1.02 us (2%)
    pallas_call x1, Pallas kernels, local(): pl.pallas_call(functools.partial(kernel, n_orb), out_shape=jax.ShapeDtype...  63 us

profile of v6, /device:TPU:135, one launch (start us, length us, event | category | flops | bytes accessed | tf_op | source)
XLA Modules:
  0.0 64.0 jit_solution(16081704227221538321)
XLA Ops:
  0.0 63.0 %shard_map.55 = bf16[4,384,384]{2,1,0:T(8,128)(2,1)S(1)} custom-call(bf16[4,384,384]{2,1,0:T(8,128)(2,1)} %b_hbm.1, bf16[1536,384]{1,0:T(8,128)(2,1)} %m_hbm.1, f32[512]{0:T(512)} %occ_hbm.1, f32[384]{0:T(512)} %vir_hbm.1, s32[2,6]{1,0:T(2,128)} %bitcast.1), custom_call_target="tpu_custom_call" | custom-call | tf_op jit(solution)/shard_map/pallas_call | solution.py:538
  63.0 1.0 %copy.7 = bf16[4,384,384]{2,1,0:T(8,128)(2,1)} copy(bf16[4,384,384]{2,1,0:T(8,128)(2,1)S(1)} %shard_map.55) | data formatting | bytes 2359296
